TPU v7x, 32 devices: a whole 2x2x4 slice. The times are simulated.
32 devices in a mesh: gx: 8 (over y, x, core), gy: 4 (over z).
Axes of the slice: x: 2, y: 2, z: 4, core: 2. Of those that a mesh axis runs over, the one named last changes fastest.
Arguments:
- source: float32 [1, 32, 128, 512], P(None, None, 'gx', 'gy'), may hold values from -6 to 6
- first_guess: float32 [1, 32, 128, 512], P(None, None, 'gx', 'gy'), may hold values from -6 to 6
- metric: float32 [128, 512], P('gx', 'gy'), may hold values from 0.5 to 2
- terrain_slope: float32 [128, 512], P('gx', 'gy'), may hold values from -6 to 6
- profile_rows: float32 [4, 32, 128], P('gy', None, 'gx'), may hold values from -6 to 6
- profile_map: int32 [4], replicated, may hold values from 0 to 3, each once
Outputs:
- multiplier: float32 [1, 32, 128, 512], P(None, None, 'gx', 'gy')
Inputs may be any that keep to these rules, and one draw needn't show every extreme that they name: `profile_map`: every row of the profile table is named exactly once.
All inputs are finite; a program needn't handle non-finite values.
Results may differ from a plain program's by a relative error of at most 0.0001.
Values sent between devices are 32-bit elements; how exact they have to be, the bound alone decides.
A program may use at most 64 MiB of HBM per device.

v0:
```python
import jax
import jax.numpy as jnp
from jax import lax
from jax.sharding import PartitionSpec as P

LEVELS = 4
COARSE = 6
CYCLES = 3


SIGMA = 0.05
WEIGHT = 0.8
VERTICAL = 4.0
ALONG_Y = 1.0


def padded_2(block, sides, width):
    for axis, dim in sides:
        count = lax.axis_size(axis)
        forward = [(i, i + 1) for i in range(count - 1)]
        backward = [(target, source) for source, target in forward]
        low = lax.ppermute(
            lax.slice_in_dim(block, block.shape[dim] - width, None, axis=dim), axis, forward
        )
        high = lax.ppermute(lax.slice_in_dim(block, 0, width, axis=dim), axis, backward)
        block = jnp.concatenate([low, block, high], axis=dim)
    return block


def level_coefficients(grid_level):
    along_x = 0.25**grid_level
    along_z = VERTICAL * along_x
    centre = SIGMA + 2.0 * along_x + 2.0 * ALONG_Y + 2.0 * along_z
    return (along_x, along_z, centre)


def apply_operator(padded_xy, metric, grid_level):
    along_x, along_z, centre = level_coefficients(grid_level)
    padded = jnp.pad(padded_xy, ((0, 0), (1, 1), (0, 0), (0, 0)))
    middle = padded[:, 1:-1, 1:-1, 1:-1]
    beside = along_x * (padded[:, 1:-1, 2:, 1:-1] + padded[:, 1:-1, :-2, 1:-1])
    beside = beside + ALONG_Y * (padded[:, 1:-1, 1:-1, 2:] + padded[:, 1:-1, 1:-1, :-2])
    beside = beside + along_z * (padded[:, 2:, 1:-1, 1:-1] + padded[:, :-2, 1:-1, 1:-1])
    return metric * (centre * middle - beside)


def relax_sweep(values, right_side, applied, metric, grid_level):
    centre = level_coefficients(grid_level)[2]
    return values + WEIGHT * (right_side - applied) / (metric * centre)


def from_zero(right_side, metric, grid_level):
    centre = level_coefficients(grid_level)[2]
    return WEIGHT * right_side / (metric * centre)


def restrict(values):
    members, depth, width, length = values.shape
    return values.reshape(members, depth // 2, 2, width // 2, 2, length).sum(axis=(2, 4)) * 0.25


def prolong(values):
    return jnp.repeat(jnp.repeat(values, 2, axis=1), 2, axis=2)


def coarsen_metric(metric):
    width, length = metric.shape
    return 0.5 * metric.reshape(width // 2, 2, length).sum(axis=1)


def halo_faces(values):
    return padded_2(values, (("gx", 2), ("gy", 3)), 1)


def sweep_faces(values):
    return padded_2(values, (("gx", 2), ("gy", 3)), 1)


def coarse_sharded(right_side, metric, grid_level):
    estimate = from_zero(right_side, metric, grid_level)
    for sweep_index in range(COARSE - 1):
        padded = padded_2(estimate, (("gx", 2), ("gy", 3)), 1)
        estimate = relax_sweep(
            estimate, right_side, apply_operator(padded, metric, grid_level), metric, grid_level
        )
    return estimate


def descend(right_side, metrics, grid_level, coarse_solve):
    if grid_level == LEVELS - 1:
        return coarse_solve(right_side, grid_level)
    metric = metrics[grid_level]
    smoothed = from_zero(right_side, metric, grid_level)
    residual = right_side - apply_operator(halo_faces(smoothed), metric, grid_level)
    correction = descend(restrict(residual), metrics, grid_level + 1, coarse_solve)
    corrected = smoothed + prolong(correction)
    applied = apply_operator(halo_faces(corrected), metric, grid_level)
    return relax_sweep(corrected, right_side, applied, metric, grid_level)


def per_device(source, first_guess, metric, terrain_slope, profile_rows, profile_map):
    gathered_rows = lax.all_gather(profile_rows, "gy", axis=0, tiled=True)
    tiles = profile_map.reshape(source.shape[0], lax.axis_size("gy"))
    wanted = lax.dynamic_slice_in_dim(tiles, lax.axis_index("gy"), 1, 1)[:, 0]
    chosen = jnp.take(gathered_rows, wanted, axis=0)
    right_side = source + chosen[:, :, :, None] * terrain_slope
    metrics = [metric]
    for grid_level in range(1, LEVELS):
        metrics.append(coarsen_metric(metrics[-1]))

    def coarse_solve(coarse_side, grid_level):
        return coarse_sharded(coarse_side, metrics[grid_level], grid_level)

    estimate = first_guess
    for cycle_number in range(CYCLES):
        first_applied = apply_operator(sweep_faces(estimate), metric, 0)
        smoothed = relax_sweep(estimate, right_side, first_applied, metric, 0)
        applied = apply_operator(sweep_faces(smoothed), metric, 0)
        residual = right_side - applied
        correction = descend(restrict(residual), metrics, 1, coarse_solve)
        corrected = smoothed + prolong(correction)
        post_applied = apply_operator(halo_faces(corrected), metric, 0)
        estimate = relax_sweep(corrected, right_side, post_applied, metric, 0)
    return estimate


def solution(mesh):
    return jax.shard_map(
        per_device,
        mesh=mesh,
        in_specs=(
            P(None, None, "gx", "gy"),
            P(None, None, "gx", "gy"),
            P("gx", "gy"),
            P("gx", "gy"),
            P("gy", None, "gx"),
            P(),
        ),
        out_specs=P(None, None, "gx", "gy"),
        check_vma=False,
    )
```

profile of v0, /device:TPU:1, one launch (start us, length us, event | category | flops | bytes accessed | tf_op | source)
XLA Modules:
  0.0 655.8 jit_solution(190604565152343912)
XLA Ops:
  1.0 4.5 collective-permute-start.1
  10.7 10.5 %all_gather.3 = f32[4,32,16]{1,2,0:T(8,128)S(1)} all-gather(f32[1,32,16]{1,2,0:T(8,128)S(1)} %copy-done.4), channel_id=1, replica_groups=mesh['gx'=8,'gy'=4] {'gy'}, dimensions={0}, use_global_device_ids=true | all-gather | bytes 10240 | tf_op jit(solution)/shard_map/all_gather | solution.py:102
  27.0 6.0 collective-permute-done.3
  33.0 3.9 collective-permute-done.2
  38.0 5.3 collective-permute-start.5
  52.6 6.1 collective-permute-done.7
  58.7 4.1 collective-permute-done.6
  77.3 3.8 collective-permute-done.10
  81.7 4.7 collective-permute-start.13
  98.5 4.2 collective-permute-start.17
  114.3 3.9 collective-permute-start.21
  129.8 3.9 collective-permute-start.25
  145.4 3.9 collective-permute-start.29
  160.9 3.9 collective-permute-start.33
  176.6 3.9 collective-permute-start.37
  192.5 3.9 collective-permute-start.41
  209.9 3.9 collective-permute-start.45
  222.5 5.7 collective-permute-done.47
  228.2 4.1 collective-permute-done.46
  245.4 5.3 collective-permute-done.51
  250.7 4.1 collective-permute-done.50
  267.7 6.1 collective-permute-done.55
  273.7 4.1 collective-permute-done.54
  290.9 4.0 collective-permute-done.58
  325.2 3.9 collective-permute-start.69
  340.7 3.9 collective-permute-start.73
  356.3 3.9 collective-permute-start.77
  371.8 3.9 collective-permute-start.81
  387.4 3.9 collective-permute-start.85
  403.4 3.9 collective-permute-start.89
  420.8 3.9 collective-permute-start.93
  433.4 5.7 collective-permute-done.95
  439.0 4.1 collective-permute-done.94
  456.1 5.5 collective-permute-done.99
  461.6 4.1 collective-permute-done.98
  478.7 5.9 collective-permute-done.103
  484.6 4.1 collective-permute-done.102
  501.8 4.0 collective-permute-done.106
  536.0 3.9 collective-permute-start.117
  551.6 3.9 collective-permute-start.121
  567.1 3.9 collective-permute-start.125
  582.7 3.9 collective-permute-start.129
  598.3 3.9 collective-permute-start.133
  614.3 3.9 collective-permute-start.137
  627.3 3.8 collective-permute-done.138
  631.7 3.9 collective-permute-start.141
  644.2 5.7 collective-permute-done.143
  649.9 4.1 collective-permute-done.142
  (488 shorter events, 435.5 us)
Async XLA Ops:
  1.0 20.1 %collective-permute-start.1 = (f32[1,32,1,128]{3,2,1,0:T(1,128)S(1)}, f32[1,32,1,128]{3,2,1,0:T(1,128)S(1)}, u32[]{:S(2)}, u32[]{:S(2)}) collective-permute-start(f32[1,32,1,128]{3,2,1,0:T(1,128)S(1)} %get-tuple-element.50), channel_id=1, source_target_pairs={{0,4},{4,8},{8,12},{12,16},{16,20},{20,24},{24,28},{1,5},{5,9},{9,... | collective-permute-start | bytes 49160 | tf_op jit(solution)/shard_map/ppermute | solution.py:22
  5.5 15.6 %collective-permute-start = (f32[1,32,1,128]{3,2,1,0:T(1,128)S(1)}, f32[1,32,1,128]{3,2,1,0:T(1,128)S(1)}, u32[]{:S(2)}, u32[]{:S(2)}) collective-permute-start(f32[1,32,1,128]{3,2,1,0:T(1,128)S(1)} %get-tuple-element.51), channel_id=1, source_target_pairs={{4,0},{8,4},{12,8},{16,12},{20,16},{24,20},{28,24},{5,1},{9,5},{13... | collective-permute-start | bytes 49160 | tf_op jit(solution)/shard_map/ppermute | solution.py:25
  22.4 10.6 %collective-permute-start.3 = (f32[1,32,18,1]{3,2,1,0:T(8,128)S(1)}, f32[1,32,18,1]{3,2,1,0:T(8,128)S(1)}, u32[]{:S(2)}, u32[]{:S(2)}) collective-permute-start(f32[1,32,18,1]{3,2,1,0:T(8,128)S(1)} %get-tuple-element.32), channel_id=1, source_target_pairs={{0,1},{1,2},{2,3},{4,5},{5,6},{6,7},{8,9},{9,10},{10,11},{12,13},{... | collective-permute-start | bytes 6920 | tf_op jit(solution)/shard_map/ppermute | solution.py:22
  25.6 11.2 %collective-permute-start.2 = (f32[1,32,18,1]{3,2,1,0:T(8,128)S(1)}, f32[1,32,18,1]{3,2,1,0:T(8,128)S(1)}, u32[]{:S(2)}, u32[]{:S(2)}) collective-permute-start(f32[1,32,18,1]{3,2,1,0:T(8,128)S(1)} %get-tuple-element.33), channel_id=1, source_target_pairs={{1,0},{2,1},{3,2},{5,4},{6,5},{7,6},{9,8},{10,9},{11,10},{13,12},{... | collective-permute-start | bytes 6920 | tf_op jit(solution)/shard_map/ppermute | solution.py:25
  38.0 7.3 %collective-permute-start.5 = (f32[1,32,1,128]{3,2,1,0:T(1,128)S(1)}, f32[1,32,1,128]{3,2,1,0:T(1,128)S(1)}, u32[]{:S(2)}, u32[]{:S(2)}) collective-permute-start(f32[1,32,1,128]{3,2,1,0:T(1,128)S(1)} %get-tuple-element.48), channel_id=1, source_target_pairs={{0,4},{4,8},{8,12},{12,16},{16,20},{20,24},{24,28},{1,5},{5,9},{9,... | collective-permute-start | bytes 49160 | tf_op jit(solution)/shard_map/ppermute | solution.py:22
  48.6 10.1 %collective-permute-start.7 = (f32[1,32,18,1]{3,2,1,0:T(8,128)S(1)}, f32[1,32,18,1]{3,2,1,0:T(8,128)S(1)}, u32[]{:S(2)}, u32[]{:S(2)}) collective-permute-start(f32[1,32,18,1]{3,2,1,0:T(8,128)S(1)} %get-tuple-element.30), channel_id=1, source_target_pairs={{0,1},{1,2},{2,3},{4,5},{5,6},{6,7},{8,9},{9,10},{10,11},{12,13},{... | collective-permute-start | bytes 6920 | tf_op jit(solution)/shard_map/ppermute | solution.py:22
  51.3 11.5 %collective-permute-start.6 = (f32[1,32,18,1]{3,2,1,0:T(8,128)S(1)}, f32[1,32,18,1]{3,2,1,0:T(8,128)S(1)}, u32[]{:S(2)}, u32[]{:S(2)}) collective-permute-start(f32[1,32,18,1]{3,2,1,0:T(8,128)S(1)} %get-tuple-element.31), channel_id=1, source_target_pairs={{1,0},{2,1},{3,2},{5,4},{6,5},{7,6},{9,8},{10,9},{11,10},{13,12},{... | collective-permute-start | bytes 6920 | tf_op jit(solution)/shard_map/ppermute | solution.py:25
  75.4 5.7 collective-permute-start.10
  81.7 6.7 %collective-permute-start.13 = (f32[1,8,1,128]{3,2,1,0:T(1,128)S(1)}, f32[1,8,1,128]{3,2,1,0:T(1,128)S(1)}, u32[]{:S(2)}, u32[]{:S(2)}) collective-permute-start(f32[1,8,1,128]{3,2,1,0:T(1,128)S(1)} %get-tuple-element.98), channel_id=1, source_target_pairs={{0,4},{4,8},{8,12},{12,16},{16,20},{20,24},{24,28},{1,5},{5,9},{9,... | collective-permute-start | bytes 12296 | tf_op jit(solution)/shard_map/ppermute | solution.py:22
  98.5 6.1 collective-permute-start.17
  114.3 5.8 collective-permute-start.21
  129.8 5.9 collective-permute-start.25
  145.4 5.9 collective-permute-start.29
  160.9 5.9 collective-permute-start.33
  176.6 5.9 collective-permute-start.37
  192.5 5.8 collective-permute-start.41
  203.6 5.7 collective-permute-start.42
  209.9 5.8 collective-permute-start.45
  219.3 8.9 %collective-permute-start.47 = (f32[1,32,18,1]{3,2,1,0:T(8,128)S(1)}, f32[1,32,18,1]{3,2,1,0:T(8,128)S(1)}, u32[]{:S(2)}, u32[]{:S(2)}) collective-permute-start(f32[1,32,18,1]{3,2,1,0:T(8,128)S(1)} %get-tuple-element.28), channel_id=1, source_target_pairs={{0,1},{1,2},{2,3},{4,5},{5,6},{6,7},{8,9},{9,10},{10,11},{12,13},{... | collective-permute-start | bytes 6920 | tf_op jit(solution)/shard_map/ppermute | solution.py:22
  221.2 11.1 %collective-permute-start.46 = (f32[1,32,18,1]{3,2,1,0:T(8,128)S(1)}, f32[1,32,18,1]{3,2,1,0:T(8,128)S(1)}, u32[]{:S(2)}, u32[]{:S(2)}) collective-permute-start(f32[1,32,18,1]{3,2,1,0:T(8,128)S(1)} %get-tuple-element.29), channel_id=1, source_target_pairs={{1,0},{2,1},{3,2},{5,4},{6,5},{7,6},{9,8},{10,9},{11,10},{13,12},{... | collective-permute-start | bytes 6920 | tf_op jit(solution)/shard_map/ppermute | solution.py:25
  242.2 8.5 %collective-permute-start.51 = (f32[1,32,18,1]{3,2,1,0:T(8,128)S(1)}, f32[1,32,18,1]{3,2,1,0:T(8,128)S(1)}, u32[]{:S(2)}, u32[]{:S(2)}) collective-permute-start(f32[1,32,18,1]{3,2,1,0:T(8,128)S(1)} %get-tuple-element.26), channel_id=1, source_target_pairs={{0,1},{1,2},{2,3},{4,5},{5,6},{6,7},{8,9},{9,10},{10,11},{12,13},{... | collective-permute-start | bytes 6920 | tf_op jit(solution)/shard_map/ppermute | solution.py:22
  243.9 10.9 %collective-permute-start.50 = (f32[1,32,18,1]{3,2,1,0:T(8,128)S(1)}, f32[1,32,18,1]{3,2,1,0:T(8,128)S(1)}, u32[]{:S(2)}, u32[]{:S(2)}) collective-permute-start(f32[1,32,18,1]{3,2,1,0:T(8,128)S(1)} %get-tuple-element.27), channel_id=1, source_target_pairs={{1,0},{2,1},{3,2},{5,4},{6,5},{7,6},{9,8},{10,9},{11,10},{13,12},{... | collective-permute-start | bytes 6920 | tf_op jit(solution)/shard_map/ppermute | solution.py:25
  265.0 8.7 %collective-permute-start.55 = (f32[1,32,18,1]{3,2,1,0:T(8,128)S(1)}, f32[1,32,18,1]{3,2,1,0:T(8,128)S(1)}, u32[]{:S(2)}, u32[]{:S(2)}) collective-permute-start(f32[1,32,18,1]{3,2,1,0:T(8,128)S(1)} %get-tuple-element.24), channel_id=1, source_target_pairs={{0,1},{1,2},{2,3},{4,5},{5,6},{6,7},{8,9},{9,10},{10,11},{12,13},{... | collective-permute-start | bytes 6920 | tf_op jit(solution)/shard_map/ppermute | solution.py:22
  266.4 11.5 %collective-permute-start.54 = (f32[1,32,18,1]{3,2,1,0:T(8,128)S(1)}, f32[1,32,18,1]{3,2,1,0:T(8,128)S(1)}, u32[]{:S(2)}, u32[]{:S(2)}) collective-permute-start(f32[1,32,18,1]{3,2,1,0:T(8,128)S(1)} %get-tuple-element.25), channel_id=1, source_target_pairs={{1,0},{2,1},{3,2},{5,4},{6,5},{7,6},{9,8},{10,9},{11,10},{13,12},{... | collective-permute-start | bytes 6920 | tf_op jit(solution)/shard_map/ppermute | solution.py:25
  289.0 6.0 collective-permute-start.58
  325.2 5.8 collective-permute-start.69
  340.7 5.9 collective-permute-start.73
  356.3 5.9 collective-permute-start.77
  371.8 5.9 collective-permute-start.81
  387.4 5.9 collective-permute-start.85
  403.4 5.8 collective-permute-start.89
  420.8 5.8 collective-permute-start.93
  430.1 8.9 %collective-permute-start.95 = (f32[1,32,18,1]{3,2,1,0:T(8,128)S(1)}, f32[1,32,18,1]{3,2,1,0:T(8,128)S(1)}, u32[]{:S(2)}, u32[]{:S(2)}) collective-permute-start(f32[1,32,18,1]{3,2,1,0:T(8,128)S(1)} %get-tuple-element.22), channel_id=1, source_target_pairs={{0,1},{1,2},{2,3},{4,5},{5,6},{6,7},{8,9},{9,10},{10,11},{12,13},{... | collective-permute-start | bytes 6920 | tf_op jit(solution)/shard_map/ppermute | solution.py:22
  432.1 11.1 %collective-permute-start.94 = (f32[1,32,18,1]{3,2,1,0:T(8,128)S(1)}, f32[1,32,18,1]{3,2,1,0:T(8,128)S(1)}, u32[]{:S(2)}, u32[]{:S(2)}) collective-permute-start(f32[1,32,18,1]{3,2,1,0:T(8,128)S(1)} %get-tuple-element.23), channel_id=1, source_target_pairs={{1,0},{2,1},{3,2},{5,4},{6,5},{7,6},{9,8},{10,9},{11,10},{13,12},{... | collective-permute-start | bytes 6920 | tf_op jit(solution)/shard_map/ppermute | solution.py:25
  453.1 8.5 %collective-permute-start.99 = (f32[1,32,18,1]{3,2,1,0:T(8,128)S(1)}, f32[1,32,18,1]{3,2,1,0:T(8,128)S(1)}, u32[]{:S(2)}, u32[]{:S(2)}) collective-permute-start(f32[1,32,18,1]{3,2,1,0:T(8,128)S(1)} %get-tuple-element.20), channel_id=1, source_target_pairs={{0,1},{1,2},{2,3},{4,5},{5,6},{6,7},{8,9},{9,10},{10,11},{12,13},{... | collective-permute-start | bytes 6920 | tf_op jit(solution)/shard_map/ppermute | solution.py:22
  454.8 10.9 %collective-permute-start.98 = (f32[1,32,18,1]{3,2,1,0:T(8,128)S(1)}, f32[1,32,18,1]{3,2,1,0:T(8,128)S(1)}, u32[]{:S(2)}, u32[]{:S(2)}) collective-permute-start(f32[1,32,18,1]{3,2,1,0:T(8,128)S(1)} %get-tuple-element.21), channel_id=1, source_target_pairs={{1,0},{2,1},{3,2},{5,4},{6,5},{7,6},{9,8},{10,9},{11,10},{13,12},{... | collective-permute-start | bytes 6920 | tf_op jit(solution)/shard_map/ppermute | solution.py:25
  475.9 8.7 %collective-permute-start.103 = (f32[1,32,18,1]{3,2,1,0:T(8,128)S(1)}, f32[1,32,18,1]{3,2,1,0:T(8,128)S(1)}, u32[]{:S(2)}, u32[]{:S(2)}) collective-permute-start(f32[1,32,18,1]{3,2,1,0:T(8,128)S(1)} %get-tuple-element.18), channel_id=1, source_target_pairs={{0,1},{1,2},{2,3},{4,5},{5,6},{6,7},{8,9},{9,10},{10,11},{12,13},{... | collective-permute-start | bytes 6920 | tf_op jit(solution)/shard_map/ppermute | solution.py:22
  477.2 11.5 %collective-permute-start.102 = (f32[1,32,18,1]{3,2,1,0:T(8,128)S(1)}, f32[1,32,18,1]{3,2,1,0:T(8,128)S(1)}, u32[]{:S(2)}, u32[]{:S(2)}) collective-permute-start(f32[1,32,18,1]{3,2,1,0:T(8,128)S(1)} %get-tuple-element.19), channel_id=1, source_target_pairs={{1,0},{2,1},{3,2},{5,4},{6,5},{7,6},{9,8},{10,9},{11,10},{13,12},{... | collective-permute-start | bytes 6920 | tf_op jit(solution)/shard_map/ppermute | solution.py:25
  499.9 6.0 collective-permute-start.106
  536.0 5.8 collective-permute-start.117
  551.6 5.9 collective-permute-start.121
  567.1 5.9 collective-permute-start.125
  582.7 5.9 collective-permute-start.129
  598.3 5.9 collective-permute-start.133
  614.3 5.8 collective-permute-start.137
  631.7 5.8 collective-permute-start.141
  641.0 8.9 %collective-permute-start.143 = (f32[1,32,18,1]{3,2,1,0:T(8,128)S(1)}, f32[1,32,18,1]{3,2,1,0:T(8,128)S(1)}, u32[]{:S(2)}, u32[]{:S(2)}) collective-permute-start(f32[1,32,18,1]{3,2,1,0:T(8,128)S(1)} %get-tuple-element.16), channel_id=1, source_target_pairs={{0,1},{1,2},{2,3},{4,5},{5,6},{6,7},{8,9},{9,10},{10,11},{12,13},{... | collective-permute-start | bytes 6920 | tf_op jit(solution)/shard_map/ppermute | solution.py:22
  642.9 11.1 %collective-permute-start.142 = (f32[1,32,18,1]{3,2,1,0:T(8,128)S(1)}, f32[1,32,18,1]{3,2,1,0:T(8,128)S(1)}, u32[]{:S(2)}, u32[]{:S(2)}) collective-permute-start(f32[1,32,18,1]{3,2,1,0:T(8,128)S(1)} %get-tuple-element.17), channel_id=1, source_target_pairs={{1,0},{2,1},{3,2},{5,4},{6,5},{7,6},{9,8},{10,9},{11,10},{13,12},{... | collective-permute-start | bytes 6920 | tf_op jit(solution)/shard_map/ppermute | solution.py:25
  (102 other events, 476.4 us)
where the time goes:
time: 661 us; the launch traced here: 656 us
  starting transfers between devices  322 us (49%)
  waiting for transfers between devices  291 us (44%)
  other arithmetic  21 us (3%)
  blocking collectives  10.5 us (2%)
  local copies, waits for them, and re-layouts  6.9 us (1%)
    ppermute x72, waiting for transfers between devices, padded_2(): lax.ppermute(lax.slice_in_dim(block, 0, width, axis=dim), axis, backward)  235 us
    ppermute x72, starting transfers between devices, padded_2(): lax.ppermute(lax.slice_in_dim(block, block.shape[dim] - width, None, axis...  206 us
    ppermute x72, starting transfers between devices, padded_2(): lax.ppermute(lax.slice_in_dim(block, 0, width, axis=dim), axis, backward)  116 us
    ppermute x72, waiting for transfers between devices, padded_2(): lax.ppermute(lax.slice_in_dim(block, block.shape[dim] - width, None, axis...  55.7 us
  transfers between devices with their start and end apart: 144, of which 86 were waited for; matrix products, arithmetic and copies ran while one was open for 0% of the time, Pallas kernels for 0%

commit v1 on v0

v1 whole, which is shorter than its diff:
```python
import jax
import jax.numpy as jnp
from jax import lax
from jax.experimental import pallas as pl
from jax.experimental.pallas import tpu as pltpu
from jax.sharding import PartitionSpec as P

CYCLES = 3
SWEEPS = 5
SIGMA = 0.05
WEIGHT = 0.8
REACH = 3
NEAR = tuple((dx, dy) for dx in (-1, 0, 1) for dy in (-1, 0, 1) if (dx, dy) != (0, 0))
FAR = tuple(
    (dx, dy) for dx in range(-REACH, REACH + 1) for dy in (-1, 0, 1) if (dx, dy) != (0, 0)
)
MESH = pl.DeviceIdType.MESH


def coefficients(grid_level):
    kx = 0.25**grid_level
    kz = 4.0 * kx
    return kx, kz, SIGMA + 2.0 * kx + 2.0 + 2.0 * kz


def loop(low, high, body, step=1):
    count = (high - low) // step

    def several(i, carry):
        for part in range(step):
            body(low + i * step + part)
        return carry

    lax.fori_loop(0, count, several, 0)
    for i in range(low + count * step, high):
        body(i)


def make_kernel(n_gx, n_gy):
    def kernel(
        source, guess, metric, slope, profile, table,
        out,
        v0, s0, g0, s1, g1, s2, r0, r1, r2, p1, p2, p3,
        m0, m1, m2, w1, w2, w3, mrx, prx, ytx, yrx, g2tx, g2rx, g3tx, g3rx,
        near_send, near_recv, metric_send, metric_recv,
        g2_send, g2_recv, g3_send, g3_recv, prof_send, prof_recv,
    ):
        gx, gy = lax.axis_index("gx"), lax.axis_index("gy")

        def there(dx, dy):
            x, y = gx + dx, gy + dy
            inside = jnp.logical_and(x >= 0, x < n_gx)
            return jnp.logical_and(inside, jnp.logical_and(y >= 0, y < n_gy))

        def device(dx, dy):
            return (gx + dx, gy + dy)

        lane = lax.broadcasted_iota(jnp.int32, (1, 128), 1)
        plus = jnp.where(gy + 1 < n_gy, 1.0, 0.0).astype(jnp.float32)
        minus = jnp.where(gy >= 1, 1.0, 0.0).astype(jnp.float32)
        halo_row = jnp.where(lane < 64, plus, minus)

        def column_in(c, per_device, first):
            position = gx * per_device + c - first
            return jnp.where(
                jnp.logical_and(position >= 0, position < n_gx * per_device), 1.0, 0.0
            ).astype(jnp.float32)

        barrier = pltpu.get_barrier_semaphore()
        total = jnp.int32(n_gy - 1)
        for o in range(1, n_gy):
            pl.semaphore_signal(
                barrier, inc=1, device_id=(gx, lax.rem(gy + o, n_gy)), device_id_type=MESH
            )
        for dx, dy in FAR:
            if dx != 0:
                present = there(dx, dy)
                total = total + jnp.where(present, 1, 0)

                @pl.when(present)
                def _():
                    pl.semaphore_signal(
                        barrier, inc=1, device_id=device(dx, dy), device_id_type=MESH
                    )

        for x in range(16):
            v0[0, 8 + x, 0, 8:40, :] = guess[pl.ds(x, 32, stride=16), :]

        def clear(ref, columns, depth, lead=()):
            zero = jnp.zeros((8, 128), jnp.float32)

            def body(c):
                for t in range(2):
                    ref[(*lead, c, t, pl.ds(0, 8), slice(None))] = zero
                    ref[(*lead, c, t, pl.ds(8 + depth, 8), slice(None))] = zero

            loop(0, columns, body, 4)

        for r in range(CYCLES):
            clear(v0, 32, 32, (r,))
        clear(s0, 32, 32)
        clear(s1, 16, 16)
        clear(s2, 8, 8)

        for i, (dx, dy) in enumerate(NEAR):
            @pl.when(jnp.logical_not(there(dx, dy)))
            def _():
                mrx[dx + 1, dy + 1] = jnp.ones((16, 128), jnp.float32)
                for r in range(CYCLES):
                    g2rx[r, dx + 1, dy + 1] = jnp.zeros((4, 8, 128), jnp.float32)
                if dy != 0:
                    for r in range(CYCLES + 1):
                        yrx[r, dx + 1, (dy + 1) // 2] = jnp.zeros((32, 128), jnp.float32)
                else:
                    first = 0 if dx < 0 else 24

                    def body(c):
                        g0[first + c, 0] = jnp.zeros((32, 128), jnp.float32)
                        for r in range(CYCLES):
                            v0[r, first + c, 0, 8:40, :] = jnp.zeros((32, 128), jnp.float32)

                    loop(0, 8, body)
        for dx, dy in FAR:
            @pl.when(jnp.logical_not(there(dx, dy)))
            def _():
                for r in range(CYCLES):
                    g3rx[r, dx + REACH, dy + 1] = jnp.zeros((8, 128), jnp.float32)

        prx[gy] = profile[0]
        mrx[1, 1] = metric[...]
        pl.semaphore_wait(barrier, total)

        def profile_copy(o):
            target = lax.rem(gy + o, n_gy)
            return pltpu.make_async_remote_copy(
                src_ref=profile.at[0], dst_ref=prx.at[gy],
                send_sem=prof_send.at[o], recv_sem=prof_recv.at[o],
                device_id=(gx, target), device_id_type=MESH,
            )

        def profile_arrival(o):
            origin = lax.rem(gy + n_gy - o, n_gy)
            return pltpu.make_async_remote_copy(
                src_ref=profile.at[0], dst_ref=prx.at[origin],
                send_sem=prof_send.at[o], recv_sem=prof_recv.at[o],
                device_id=(gx, origin), device_id_type=MESH,
            )

        for o in range(1, n_gy):
            profile_copy(o).start()

        def near_copy(r, i, arriving, is_g):
            dx, dy = NEAR[i]
            sx, sy = (dx, dy) if arriving else (-dx, -dy)
            slot = i if arriving else len(NEAR) - 1 - i
            if dy == 0:
                here = 8 if dx < 0 else 16
                land = 0 if sx < 0 else 24
                if is_g:
                    src = g0.at[pl.ds(here, 8), 0]
                    dst = g0.at[pl.ds(land, 8), 0]
                else:
                    src = v0.at[r, pl.ds(here, 8), 0, pl.ds(8, 32), :]
                    dst = v0.at[r, pl.ds(land, 8), 0, pl.ds(8, 32), :]
            else:
                src = ytx.at[r]
                dst = yrx.at[r, sx + 1, (sy + 1) // 2]
            return pltpu.make_async_remote_copy(
                src_ref=src, dst_ref=dst,
                send_sem=near_send.at[r, i], recv_sem=near_recv.at[r, slot],
                device_id=device(dx, dy), device_id_type=MESH,
            )

        def block_copy(kind, r, dx, dy, i, count, arriving):
            sx, sy = (dx, dy) if arriving else (-dx, -dy)
            slot = i if arriving else count - 1 - i
            if kind == "m":
                src, dst = metric, mrx.at[sx + 1, sy + 1]
                ss, rs = metric_send.at[i], metric_recv.at[slot]
            elif kind == "g2":
                src, dst = g2tx.at[r], g2rx.at[r, sx + 1, sy + 1]
                ss, rs = g2_send.at[r, i], g2_recv.at[r, slot]
            else:
                src, dst = g3tx.at[r], g3rx.at[r, sx + REACH, sy + 1]
                ss, rs = g3_send.at[r, i], g3_recv.at[r, slot]
            return pltpu.make_async_remote_copy(
                src_ref=src, dst_ref=dst, send_sem=ss, recv_sem=rs,
                device_id=device(dx, dy), device_id_type=MESH,
            )

        def when_there(dx, dy, action):
            @pl.when(there(dx, dy))
            def _():
                action()

        def start_x(r, is_g):
            for i, (dx, dy) in enumerate(NEAR):
                if dy == 0:
                    when_there(dx, dy, lambda: near_copy(r, i, False, is_g).start())

        def start_y(r, load, is_g):
            packed = jnp.zeros((32, 128), jnp.float32)
            for k in range(16):
                turned = pltpu.roll(load(k), (8 * k + 4) % 128, 1)
                packed = jnp.where(lane // 8 == k, turned, packed)
            ytx[r] = packed
            for i, (dx, dy) in enumerate(NEAR):
                if dy != 0:
                    when_there(dx, dy, lambda: near_copy(r, i, False, is_g).start())

        def wait_near(r, is_g):
            for i, (dx, dy) in enumerate(NEAR):
                when_there(dx, dy, lambda: near_copy(r, i, True, is_g).wait_recv())

        def unpack(r, store):
            for dx, first, k0, n in ((-1, 0, 8, 8), (0, 8, 0, 16), (1, 24, 0, 8)):
                both = jnp.where(lane % 8 < 4, yrx[r, dx + 1, 0], yrx[r, dx + 1, 1])
                for j in range(n):
                    shift = (128 - (8 * (k0 + j) + 4)) % 128
                    store(first + j, pltpu.roll(both, shift, 1))

        start_x(0, False)
        for i, (dx, dy) in enumerate(NEAR):
            when_there(
                dx, dy, lambda: block_copy("m", 0, dx, dy, i, len(NEAR), False).start()
            )
        start_y(0, lambda k: v0[0, 8 + k, 0, 8:40, :], False)

        centre0 = coefficients(0)[2]
        for o in range(1, n_gy):
            profile_arrival(o).wait_recv()
        chosen = prx[table[gy]]
        for x in range(16):
            f = source[pl.ds(x, 32, stride=16), :] + chosen[:, x : x + 1] * slope[x : x + 1, :]
            g0[8 + x, 0] = f * (WEIGHT / (metric[x : x + 1, :] * centre0))
        start_x(CYCLES, True)
        start_y(CYCLES, lambda k: g0[8 + k, 0], True)

        for i, (dx, dy) in enumerate(NEAR):
            when_there(
                dx, dy, lambda: block_copy("m", 0, dx, dy, i, len(NEAR), True).wait_recv()
            )
        for c in range(2, 30):
            dx, k = (c - 8) // 16, (c - 8) % 16
            m0[c, 0:1, :] = mrx[dx + 1, 1, k : k + 1, :]
            m0[c, 1:2, :] = jnp.where(
                lane < 64, mrx[dx + 1, 2, k : k + 1, :], mrx[dx + 1, 0, k : k + 1, :]
            )
        for fine, coarse, weights, level, first, span, low, high in (
            (m0, m1, w1, 1, 4, 8, 1, 15),
            (m1, m2, w2, 2, 2, 4, 1, 7),
            (m2, None, w3, 3, 1, 2, 1, 3),
        ):
            centre = coefficients(level)[2]
            for c in range(low, high):
                for t in range(2):
                    row = 0.5 * (
                        fine[2 * c, t : t + 1, :] + fine[2 * c + 1, t : t + 1, :]
                    )
                    if coarse is not None:
                        coarse[c, t : t + 1, :] = row
                    valid = column_in(c, span, first)
                    if t == 1:
                        valid = valid * halo_row
                    weights[c, t : t + 1, :] = valid * (WEIGHT / (row * centre))

        def around(ref, c, depth, grid_level, lead=(), halo=True):
            kx, kz, _ = coefficients(grid_level)

            def at(column, t, shift=0):
                return ref[(*lead, column, t, pl.ds(8 + shift, depth), slice(None))]

            mid, side = at(c, 0), at(c, 1)
            a, b = pltpu.roll(mid, 1, 1), pltpu.roll(side, 1, 1)
            p, q = pltpu.roll(mid, 127, 1), pltpu.roll(side, 127, 1)
            ys = (
                jnp.where(lane == 0, b, a) + jnp.where(lane == 127, q, p),
                jnp.where(lane == 0, a, b) + jnp.where(lane == 127, p, q) if halo else None,
            )
            result = []
            for t in range(2 if halo else 1):
                total = kx * (at(c - 1, t) + at(c + 1, t)) + ys[t]
                total = total + kz * (at(c, t, -1) + at(c, t, 1))
                result.append(((mid, side)[t], total))
            return result

        def weight_of(t, valid, grid_level):
            scale = (WEIGHT / coefficients(grid_level)[2]) * valid
            return scale if t == 0 else scale * halo_row

        def unpack_g(c, value):
            g0[c, 1] = value

        wait_near(CYCLES, True)
        unpack(CYCLES, unpack_g)

        sub = lax.broadcasted_iota(jnp.int32, (8, 128), 0)

        def cycle(r, carry):
            c0, c1, c2, c3 = (coefficients(level)[2] for level in range(4))
            wait_near(r, False)

            def unpack_v(c, value):
                v0[r, c, 1, 8:40, :] = value

            unpack(r, unpack_v)

            def sweep0(c):
                valid = column_in(c, 16, 8)
                for t, (value, nb) in enumerate(around(v0, c, 32, 0, (r,))):
                    s0[c, t, 8:40, :] = 0.2 * value + weight_of(t, valid, 0) * nb + g0[c, t]

            loop(1, 31, sweep0, 2)

            def residual0(c):
                parts = [0.0, 0.0]
                for k in range(2):
                    for t, (value, nb) in enumerate(around(s0, 2 * c + k, 32, 0)):
                        inner = c0 * (1.25 * g0[2 * c + k, t] - value) + nb
                        parts[t] = parts[t] + m0[2 * c + k, t : t + 1, :] * inner
                for t in range(2):
                    r0[c, t] = parts[t]

            loop(1, 15, residual0)

            def restrict0(c):
                for t in range(2):
                    f = r0[c, t, pl.ds(0, 16, stride=2), :] + r0[c, t, pl.ds(1, 16, stride=2), :]
                    g = f * (0.25 * w1[c, t : t + 1, :])
                    g1[c, t] = g
                    s1[c, t, 8:24, :] = g

            loop(1, 15, restrict0, 2)

            def residual1(c):
                parts = [0.0, 0.0]
                for k in range(2):
                    for t, (value, nb) in enumerate(around(s1, 2 * c + k, 16, 1)):
                        inner = (0.25 * c1) * value + nb
                        parts[t] = parts[t] + m1[2 * c + k, t : t + 1, :] * inner
                for t in range(2):
                    r1[c, t] = parts[t]

            loop(1, 7, residual1)

            def restrict1(c):
                for t in range(2):
                    f = r1[c, t, pl.ds(0, 8, stride=2), :] + r1[c, t, pl.ds(1, 8, stride=2), :]
                    s2[c, t, 8:16, :] = f * (0.25 * w2[c, t : t + 1, :])

            for c in range(1, 7):
                restrict1(c)
            for k in range(4):
                own = s2[2 + k, 0, 8:16, :]
                g2tx[r, k] = own
                g2rx[r, 1, 1, k] = own
            for i, (dx, dy) in enumerate(NEAR):
                when_there(
                    dx, dy, lambda: block_copy("g2", r, dx, dy, i, len(NEAR), False).start()
                )
            for c in range(1, 3):
                part = 0.0
                for k in range(2):
                    ((value, nb),) = around(s2, 2 * c + k, 8, 2, halo=False)
                    inner = (0.25 * c2) * value + nb
                    part = part + m2[2 * c + k, 0:1, :] * inner
                r2[c - 1] = part
                f = r2[c - 1, pl.ds(0, 4, stride=2), :] + r2[c - 1, pl.ds(1, 4, stride=2), :]
                g = f * (0.25 * w3[c, 0:1, :])
                g3tx[r, 4 * c - 4 : 4 * c, :] = g
                g3rx[r, REACH, 1, 4 * c - 4 : 4 * c, :] = g
            for i, (dx, dy) in enumerate(FAR):
                when_there(
                    dx, dy, lambda: block_copy("g3", r, dx, dy, i, len(FAR), False).start()
                )
            for i, (dx, dy) in enumerate(FAR):
                when_there(
                    dx, dy, lambda: block_copy("g3", r, dx, dy, i, len(FAR), True).wait_recv()
                )

            kx, kz, _ = coefficients(3)
            width = 2 * REACH + 1
            scale3 = []
            gs = []
            for d in range(width):
                there_x = jnp.logical_and(gx + d - REACH >= 0, gx + d - REACH < n_gx)
                valid = jnp.where(there_x, WEIGHT / c3, 0.0).astype(jnp.float32)
                scale3.append((valid, valid * halo_row))
                gs.append(
                    (g3rx[r, d, 1], jnp.where(lane < 64, g3rx[r, d, 2], g3rx[r, d, 0]))
                )
            zero = jnp.zeros((8, 128), jnp.float32)
            vs = gs
            for sweep in range(SWEEPS):
                new = []
                for d in range(width):
                    mid, side = vs[d]
                    a, b = pltpu.roll(mid, 1, 1), pltpu.roll(side, 1, 1)
                    p, q = pltpu.roll(mid, 127, 1), pltpu.roll(side, 127, 1)
                    ys = (
                        jnp.where(lane == 0, b, a) + jnp.where(lane == 127, q, p),
                        jnp.where(lane == 0, a, b) + jnp.where(lane == 127, p, q),
                    )
                    pair = []
                    for t in range(2):
                        v = vs[d][t]
                        before = vs[d - 1][t] if d > 0 else zero
                        after = vs[d + 1][t] if d + 1 < width else zero
                        xs = pltpu.roll(v + jnp.where(sub >= 4, before, after), 4, 0)
                        zs = jnp.where(sub % 4 != 0, pltpu.roll(v, 1, 0), 0.0)
                        zs = zs + jnp.where(sub % 4 != 3, pltpu.roll(v, 7, 0), 0.0)
                        nb = kx * xs + ys[t] + kz * zs
                        pair.append(0.2 * v + scale3[d][t] * nb + gs[d][t])
                    new.append(tuple(pair))
                vs = new
            for c in range(4):
                d, k = REACH + (c + 1) // 2 - 1, (c + 1) % 2
                for t in range(2):
                    column = vs[d][t][4 * k : 4 * k + 4, :]
                    p3[c, t, pl.ds(0, 4, stride=2), :] = column
                    p3[c, t, pl.ds(1, 4, stride=2), :] = column

            for i, (dx, dy) in enumerate(NEAR):
                when_there(
                    dx, dy, lambda: block_copy("g2", r, dx, dy, i, len(NEAR), True).wait_recv()
                )

            def g2_of(c):
                dx, k = (c - 2) // 4, (c - 2) % 4
                return (
                    g2rx[r, dx + 1, 1, k],
                    jnp.where(lane < 64, g2rx[r, dx + 1, 2, k], g2rx[r, dx + 1, 0, k]),
                )

            for c in range(8):
                g = g2_of(c)
                for t in range(2):
                    s2[c, t, 8:16, :] = g[t] + p3[c // 2, t]
            for c in range(1, 7):
                valid = column_in(c, 4, 2)
                g = g2_of(c)
                for t, (value, nb) in enumerate(around(s2, c, 8, 2)):
                    new = 0.2 * value + weight_of(t, valid, 2) * nb + g[t]
                    p2[c, t, pl.ds(0, 8, stride=2), :] = new
                    p2[c, t, pl.ds(1, 8, stride=2), :] = new

            def correct1(c):
                for k in range(2):
                    for t in range(2):
                        s1[2 * c + k, t, 8:24, :] = g1[2 * c + k, t] + p2[c, t]

            loop(1, 7, correct1, 2)

            def post1(c):
                valid = column_in(c, 8, 4)
                for t, (value, nb) in enumerate(around(s1, c, 16, 1)):
                    new = 0.2 * value + weight_of(t, valid, 1) * nb + g1[c, t]
                    p1[c, t, pl.ds(0, 16, stride=2), :] = new
                    p1[c, t, pl.ds(1, 16, stride=2), :] = new

            loop(3, 13, post1, 2)

            def correct0(c):
                for k in range(2):
                    for t in range(2):
                        old = s0[2 * c + k, t, 8:40, :]
                        s0[2 * c + k, t, 8:40, :] = old + p1[c, t]

            loop(3, 13, correct0)

            def post0(c):
                ((value, nb),) = around(s0, c, 32, 0, halo=False)
                v0[r + 1, c, 0, 8:40, :] = 0.2 * value + (WEIGHT / c0) * nb + g0[c, 0]

            loop(8, 24, post0, 2)

            @pl.when(r + 1 < CYCLES)
            def _():
                start_x(r + 1, False)
                start_y(r + 1, lambda k: v0[r + 1, 8 + k, 0, 8:40, :], False)

            return carry

        lax.fori_loop(0, CYCLES, cycle, 0)

        for x in range(16):
            out[pl.ds(x, 32, stride=16), :] = v0[CYCLES, 8 + x, 0, 8:40, :]

        for o in range(1, n_gy):
            profile_copy(o).wait_send()
        for i, (dx, dy) in enumerate(NEAR):
            def leave():
                block_copy("m", 0, dx, dy, i, len(NEAR), False).wait_send()
                for r in range(CYCLES + 1):
                    near_copy(r, i, False, r == CYCLES).wait_send()
                for r in range(CYCLES):
                    block_copy("g2", r, dx, dy, i, len(NEAR), False).wait_send()

            when_there(dx, dy, leave)
        for i, (dx, dy) in enumerate(FAR):
            def leave():
                for r in range(CYCLES):
                    block_copy("g3", r, dx, dy, i, len(FAR), False).wait_send()

            when_there(dx, dy, leave)

    return kernel


def solution(mesh):
    n_gx, n_gy = mesh.shape["gx"], mesh.shape["gy"]
    f32 = jnp.float32
    near, far = len(NEAR), len(FAR)
    dma = pltpu.SemaphoreType.DMA
    vmem = pl.BlockSpec(memory_space=pltpu.VMEM)
    shapes = [
        (CYCLES + 1, 32, 2, 48, 128),
        (32, 2, 48, 128),
        (32, 2, 32, 128),
        (16, 2, 32, 128),
        (16, 2, 16, 128),
        (8, 2, 24, 128),
        (16, 2, 32, 128),
        (8, 2, 16, 128),
        (2, 8, 128),
        (16, 2, 32, 128),
        (8, 2, 16, 128),
        (4, 2, 8, 128),
        (32, 8, 128),
        (16, 8, 128),
        (8, 8, 128),
        (16, 8, 128),
        (8, 8, 128),
        (4, 8, 128),
        (3, 3, 16, 128),
        (n_gy, 32, 16),
        (CYCLES + 1, 32, 128),
        (CYCLES + 1, 3, 2, 32, 128),
        (CYCLES, 4, 8, 128),
        (CYCLES, 3, 3, 4, 8, 128),
        (CYCLES, 8, 128),
        (CYCLES, 2 * REACH + 1, 3, 8, 128),
    ]
    sems = [
        dma((CYCLES + 1, near)), dma((CYCLES + 1, near)), dma((near,)), dma((near,)),
        dma((CYCLES, near)), dma((CYCLES, near)), dma((CYCLES, far)), dma((CYCLES, far)),
        dma((n_gy,)), dma((n_gy,)),
    ]
    call = pl.pallas_call(
        make_kernel(n_gx, n_gy),
        out_shape=jax.ShapeDtypeStruct((512, 128), f32),
        in_specs=[vmem] * 5 + [pl.BlockSpec(memory_space=pltpu.SMEM)],
        out_specs=vmem,
        scratch_shapes=[pltpu.VMEM(shape, f32) for shape in shapes] + sems,
        compiler_params=pltpu.CompilerParams(
            collective_id=0, has_side_effects=True, vmem_limit_bytes=40 * 1024 * 1024
        ),
    )

    def per_device(source, first_guess, metric, terrain_slope, profile_rows, profile_map):
        result = call(
            source.reshape(512, 128), first_guess.reshape(512, 128),
            metric, terrain_slope, profile_rows, profile_map,
        )
        return result.reshape(source.shape)

    return jax.shard_map(
        per_device,
        mesh=mesh,
        in_specs=(
            P(None, None, "gx", "gy"),
            P(None, None, "gx", "gy"),
            P("gx", "gy"),
            P("gx", "gy"),
            P("gy", None, "gx"),
            P(),
        ),
        out_specs=P(None, None, "gx", "gy"),
        check_vma=False,
    )
```

time: 661 us -> 61.6 us (0.09)
  starting transfers between devices: 322 us -> 0 us
  waiting for transfers between devices: 291 us -> 0 us
  Pallas kernels: 0 us -> 57.9 us
  other arithmetic: 21 us -> 0 us
  blocking collectives: 10.5 us -> 0 us
    ppermute x144 -> x0, starting transfers between devices: 322 us -> none  [the longest x72 206 us: padded_2(): lax.ppermute(lax.slice_in_dim(block, block.shape[dim] - width, None, axis...]
    ppermute x144 -> x0, waiting for transfers between devices: 291 us -> none  [the longest x72 235 us: padded_2(): lax.ppermute(lax.slice_in_dim(block, 0, width, axis=dim), axis, backward)]
    pallas_call x0 -> x1, Pallas kernels: none -> 57.9 us  [per_device(): call(source.reshape(512, 128), first_guess.reshape(512, 128), metric, ter...]
    all_gather x1 -> x0, blocking collectives: 10.5 us -> none  [per_device(): gathered_rows = lax.all_gather(profile_rows, 'gy', axis=0, tiled=True)]
    concatenate x72 -> x0, other arithmetic: 10.1 us -> none  [padded_2(): block = jnp.concatenate([low, block, high], axis=dim)]
    add x36 -> x0, other arithmetic: 7.09 us -> none  [the longest x27 6.9 us: relax_sweep(): return values + WEIGHT * (right_side - applied) / (metric * centre)]
  transfers between devices with their start and end apart: 144 -> 0, of which waited for: 86 -> 0; matrix products, arithmetic and copies ran while one was open for 0% -> 0% of each run, Pallas kernels for 0% -> 0%
where the time goes in v1:
time: 61.6 us; the launch traced here: 61.4 us
  Pallas kernels  57.9 us (94%)
  local copies, waits for them, and re-layouts  3.42 us (6%)
    pallas_call x1, Pallas kernels, per_device(): call(source.reshape(512, 128), first_guess.reshape(512, 128), metric, ter...  57.9 us
    unnamed x12, local copies, waits for them, and re-layouts  3.42 us

profile of v1, /device:TPU:1, one launch (start us, length us, event | category | flops | bytes accessed | tf_op | source)
XLA Modules:
  0.0 61.4 jit_solution(10573739250114721328)
XLA Ops:
  0.0 0.0 copy-start.2
  0.0 0.0 copy-start.3
  0.0 0.0 copy-start.4
  0.0 0.8 %copy.7.profile = f32[1,32,16]{2,1,0:T(8,128)S(1)} copy(f32[1,32,16]{1,2,0:T(8,128)} %param.10) | data formatting | bytes 4096 | tf_op args[4]
  0.8 0.0 copy-done.2
  0.8 0.0 copy-done.3
  0.8 0.0 copy-done.4
  0.8 0.0 copy-start
  0.8 0.9 %copy-done = f32[1,32,16,128]{3,2,1,0:T(8,128)S(1)} copy-done((f32[1,32,16,128]{3,2,1,0:T(8,128)S(1)}, f32[1,32,16,128]{3,2,1,0:T(8,128)}, u32[]{:S(2)}) %copy-start) | copy-done | bytes 262168
  1.8 0.0 copy-start.1
  1.8 0.9 %copy-done.1 = f32[1,32,16,128]{3,2,1,0:T(8,128)S(1)} copy-done((f32[1,32,16,128]{3,2,1,0:T(8,128)S(1)}, f32[1,32,16,128]{3,2,1,0:T(8,128)}, u32[]{:S(2)}) %copy-start.1) | copy-done | bytes 262168
  2.7 57.9 %shard_map.64 = f32[512,128]{1,0:T(8,128)S(1)} custom-call(f32[512,128]{1,0:T(8,128)S(1)} %bitcast.4, f32[512,128]{1,0:T(8,128)S(1)} %bitcast.5, f32[16,128]{1,0:T(8,128)S(1)} %copy-done.2, f32[16,128]{1,0:T(8,128)S(1)} %copy-done.3, f32[1,32,16]{2,1,0:T(8,128)S(1)} %copy.7.profile, s32[4]{0:T(128)S(1)} %copy-done.4), custom_call_target="tpu_custom_call" | custom-call | tf_op jit(solution)/shard_map/pallas_call | solution.py:561
  60.7 0.7 %copy.9 = f32[1,32,16,128]{3,2,1,0:T(8,128)} copy(f32[1,32,16,128]{3,2,1,0:T(8,128)S(1)} %bitcast.3) | data formatting | bytes 524288
Async XLA Ops:
  0.0 0.8 %copy-start.2 = (f32[16,128]{1,0:T(8,128)S(1)}, f32[16,128]{1,0:T(8,128)}, u32[]{:S(2)}) copy-start(f32[16,128]{1,0:T(8,128)} %metric.1) | copy-start | bytes 24580
  0.0 0.8 %copy-start.3 = (f32[16,128]{1,0:T(8,128)S(1)}, f32[16,128]{1,0:T(8,128)}, u32[]{:S(2)}) copy-start(f32[16,128]{1,0:T(8,128)} %slope.1) | copy-start | bytes 24580
  0.0 0.8 %copy-start.4 = (s32[4]{0:T(128)S(1)}, s32[4]{0:T(128)}, u32[]{:S(2)}) copy-start(s32[4]{0:T(128)} %table.1) | copy-start | bytes 52
  0.8 1.0 %copy-start = (f32[1,32,16,128]{3,2,1,0:T(8,128)S(1)}, f32[1,32,16,128]{3,2,1,0:T(8,128)}, u32[]{:S(2)}) copy-start(f32[1,32,16,128]{3,2,1,0:T(8,128)} %param.6) | copy-start | bytes 786436
  1.8 0.9 %copy-start.1 = (f32[1,32,16,128]{3,2,1,0:T(8,128)S(1)}, f32[1,32,16,128]{3,2,1,0:T(8,128)}, u32[]{:S(2)}) copy-start(f32[1,32,16,128]{3,2,1,0:T(8,128)} %param.7) | copy-start | bytes 786436

commit v2 on v1

--- a/solution.py
+++ b/solution.py
@@ -40,10 +40,11 @@
     def kernel(
         source, guess, metric, slope, profile, table,
         out,
-        v0, s0, g0, s1, g1, s2, r0, r1, r2, p1, p2, p3,
-        m0, m1, m2, w1, w2, w3, mrx, prx, ytx, yrx, g2tx, g2rx, g3tx, g3rx,
+        v0, s0, f0, g0, s1, g1, s2, r0, r1, r2, p1, p2, p3,
+        m0, m1, m2, w1, w2, w3, mtx, mrx, ptx, prx, ytx, yrx, gtx, grx,
+        guess_here, source_here,
         near_send, near_recv, metric_send, metric_recv,
-        g2_send, g2_recv, g3_send, g3_recv, prof_send, prof_recv,
+        g_send, g_recv, prof_send, prof_recv, local,
     ):
         gx, gy = lax.axis_index("gx"), lax.axis_index("gy")
 
@@ -66,14 +67,30 @@
                 jnp.logical_and(position >= 0, position < n_gx * per_device), 1.0, 0.0
             ).astype(jnp.float32)
 
+        guess_copy = pltpu.make_async_copy(guess, guess_here, local.at[0])
+        source_copy = pltpu.make_async_copy(source, source_here, local.at[1])
+        guess_copy.start()
+        source_copy.start()
+
         barrier = pltpu.get_barrier_semaphore()
         total = jnp.int32(n_gy - 1)
         for o in range(1, n_gy):
             pl.semaphore_signal(
                 barrier, inc=1, device_id=(gx, lax.rem(gy + o, n_gy)), device_id_type=MESH
             )
+        for dx in (-1, 1):
+            present = there(dx, 0)
+            total = total + jnp.where(present, n_gy, 0)
+
+            @pl.when(present)
+            def _():
+                for o in range(n_gy):
+                    pl.semaphore_signal(
+                        barrier, inc=1, device_id=(gx + dx, lax.rem(gy + o, n_gy)),
+                        device_id_type=MESH,
+                    )
         for dx, dy in FAR:
-            if dx != 0:
+            if abs(dx) > 1:
                 present = there(dx, dy)
                 total = total + jnp.where(present, 1, 0)
 
@@ -83,9 +100,6 @@
                         barrier, inc=1, device_id=device(dx, dy), device_id_type=MESH
                     )
 
-        for x in range(16):
-            v0[0, 8 + x, 0, 8:40, :] = guess[pl.ds(x, 32, stride=16), :]
-
         def clear(ref, columns, depth, lead=()):
             zero = jnp.zeros((8, 128), jnp.float32)
 
@@ -94,20 +108,12 @@
                     ref[(*lead, c, t, pl.ds(0, 8), slice(None))] = zero
                     ref[(*lead, c, t, pl.ds(8 + depth, 8), slice(None))] = zero
 
-            loop(0, columns, body, 4)
-
-        for r in range(CYCLES):
-            clear(v0, 32, 32, (r,))
-        clear(s0, 32, 32)
-        clear(s1, 16, 16)
-        clear(s2, 8, 8)
+            loop(0, columns, body, 8)
 
         for i, (dx, dy) in enumerate(NEAR):
             @pl.when(jnp.logical_not(there(dx, dy)))
             def _():
-                mrx[dx + 1, dy + 1] = jnp.ones((16, 128), jnp.float32)
-                for r in range(CYCLES):
-                    g2rx[r, dx + 1, dy + 1] = jnp.zeros((4, 8, 128), jnp.float32)
+                mrx[dx + 1, dy + 1] = jnp.ones((32, 128), jnp.float32)
                 if dy != 0:
                     for r in range(CYCLES + 1):
                         yrx[r, dx + 1, (dy + 1) // 2] = jnp.zeros((32, 128), jnp.float32)
@@ -115,39 +121,46 @@
                     first = 0 if dx < 0 else 24
 
                     def body(c):
-                        g0[first + c, 0] = jnp.zeros((32, 128), jnp.float32)
+                        f0[first + c, 0] = jnp.zeros((32, 128), jnp.float32)
                         for r in range(CYCLES):
                             v0[r, first + c, 0, 8:40, :] = jnp.zeros((32, 128), jnp.float32)
 
                     loop(0, 8, body)
+                    prx[dx + 1] = jnp.zeros((n_gy, 32, 16), jnp.float32)
         for dx, dy in FAR:
             @pl.when(jnp.logical_not(there(dx, dy)))
             def _():
                 for r in range(CYCLES):
-                    g3rx[r, dx + REACH, dy + 1] = jnp.zeros((8, 128), jnp.float32)
-
-        prx[gy] = profile[0]
-        mrx[1, 1] = metric[...]
+                    grx[r, dx + REACH, dy + 1] = jnp.zeros((40, 128), jnp.float32)
+
+        ptx[...] = profile[0].T
+        prx[1, gy] = ptx[...]
+        mtx[0:16, :] = metric[...]
+        mtx[16:32, :] = slope[...]
+        mrx[1, 1] = mtx[...]
+        guess_copy.wait()
+        for x in range(16):
+            v0[0, 8 + x, 0, 8:40, :] = guess_here[pl.ds(x, 32, stride=16), :]
+        source_copy.wait()
+        for x in range(16):
+            f0[8 + x, 0] = source_here[pl.ds(x, 32, stride=16), :]
         pl.semaphore_wait(barrier, total)
 
-        def profile_copy(o):
-            target = lax.rem(gy + o, n_gy)
+        def profile_copy(dx, o, arriving):
+            other = lax.rem(gy + (n_gy - o if arriving else o), n_gy)
+            sx, sy = (dx, other) if arriving else (-dx, gy)
             return pltpu.make_async_remote_copy(
-                src_ref=profile.at[0], dst_ref=prx.at[gy],
-                send_sem=prof_send.at[o], recv_sem=prof_recv.at[o],
-                device_id=(gx, target), device_id_type=MESH,
-            )
-
-        def profile_arrival(o):
-            origin = lax.rem(gy + n_gy - o, n_gy)
-            return pltpu.make_async_remote_copy(
-                src_ref=profile.at[0], dst_ref=prx.at[origin],
-                send_sem=prof_send.at[o], recv_sem=prof_recv.at[o],
-                device_id=(gx, origin), device_id_type=MESH,
-            )
-
-        for o in range(1, n_gy):
-            profile_copy(o).start()
+                src_ref=ptx, dst_ref=prx.at[sx + 1, sy],
+                send_sem=prof_send.at[dx + 1, o], recv_sem=prof_recv.at[sx + 1, o],
+                device_id=(gx + dx, other), device_id_type=MESH,
+            )
+
+        def profile_all(action):
+            for dx in (-1, 0, 1):
+                @pl.when(there(dx, 0))
+                def _():
+                    for o in range(1 if dx == 0 else 0, n_gy):
+                        action(dx, o)
 
         def near_copy(r, i, arriving, is_g):
             dx, dy = NEAR[i]
@@ -157,8 +170,8 @@
                 here = 8 if dx < 0 else 16
                 land = 0 if sx < 0 else 24
                 if is_g:
-                    src = g0.at[pl.ds(here, 8), 0]
-                    dst = g0.at[pl.ds(land, 8), 0]
+                    src = f0.at[pl.ds(here, 8), 0]
+                    dst = f0.at[pl.ds(land, 8), 0]
                 else:
                     src = v0.at[r, pl.ds(here, 8), 0, pl.ds(8, 32), :]
                     dst = v0.at[r, pl.ds(land, 8), 0, pl.ds(8, 32), :]
@@ -175,14 +188,12 @@
             sx, sy = (dx, dy) if arriving else (-dx, -dy)
             slot = i if arriving else count - 1 - i
             if kind == "m":
-                src, dst = metric, mrx.at[sx + 1, sy + 1]
+                src, dst = mtx, mrx.at[sx + 1, sy + 1]
                 ss, rs = metric_send.at[i], metric_recv.at[slot]
-            elif kind == "g2":
-                src, dst = g2tx.at[r], g2rx.at[r, sx + 1, sy + 1]
-                ss, rs = g2_send.at[r, i], g2_recv.at[r, slot]
             else:
-                src, dst = g3tx.at[r], g3rx.at[r, sx + REACH, sy + 1]
-                ss, rs = g3_send.at[r, i], g3_recv.at[r, slot]
+                rows = pl.ds(0, 40) if abs(dx) < 2 else pl.ds(32, 8)
+                src, dst = gtx.at[r, rows], grx.at[r, sx + REACH, sy + 1, rows]
+                ss, rs = g_send.at[r, i], g_recv.at[r, slot]
             return pltpu.make_async_remote_copy(
                 src_ref=src, dst_ref=dst, send_sem=ss, recv_sem=rs,
                 device_id=device(dx, dy), device_id_type=MESH,
@@ -193,9 +204,9 @@
             def _():
                 action()
 
-        def start_x(r, is_g):
+        def start_x(r, is_g, sides=(-1, 1)):
             for i, (dx, dy) in enumerate(NEAR):
-                if dy == 0:
+                if dy == 0 and dx in sides:
                     when_there(dx, dy, lambda: near_copy(r, i, False, is_g).start())
 
         def start_y(r, load, is_g):
@@ -208,39 +219,42 @@
                 if dy != 0:
                     when_there(dx, dy, lambda: near_copy(r, i, False, is_g).start())
 
-        def wait_near(r, is_g):
+        def wait_near(r, is_g, direct=None):
             for i, (dx, dy) in enumerate(NEAR):
+                if direct is not None and direct != (dx == 0):
+                    continue
                 when_there(dx, dy, lambda: near_copy(r, i, True, is_g).wait_recv())
 
-        def unpack(r, store):
+        def unpack(r, store, parts=(-1, 0, 1)):
             for dx, first, k0, n in ((-1, 0, 8, 8), (0, 8, 0, 16), (1, 24, 0, 8)):
+                if dx not in parts:
+                    continue
                 both = jnp.where(lane % 8 < 4, yrx[r, dx + 1, 0], yrx[r, dx + 1, 1])
                 for j in range(n):
                     shift = (128 - (8 * (k0 + j) + 4)) % 128
                     store(first + j, pltpu.roll(both, shift, 1))
 
         start_x(0, False)
+        start_x(CYCLES, True)
+        profile_all(lambda dx, o: profile_copy(dx, o, False).start())
         for i, (dx, dy) in enumerate(NEAR):
             when_there(
                 dx, dy, lambda: block_copy("m", 0, dx, dy, i, len(NEAR), False).start()
             )
         start_y(0, lambda k: v0[0, 8 + k, 0, 8:40, :], False)
-
-        centre0 = coefficients(0)[2]
-        for o in range(1, n_gy):
-            profile_arrival(o).wait_recv()
-        chosen = prx[table[gy]]
-        for x in range(16):
-            f = source[pl.ds(x, 32, stride=16), :] + chosen[:, x : x + 1] * slope[x : x + 1, :]
-            g0[8 + x, 0] = f * (WEIGHT / (metric[x : x + 1, :] * centre0))
-        start_x(CYCLES, True)
-        start_y(CYCLES, lambda k: g0[8 + k, 0], True)
+        start_y(CYCLES, lambda k: f0[8 + k, 0], True)
+
+        for r in range(CYCLES):
+            clear(v0, 32, 32, (r,))
+        clear(s0, 32, 32)
+        clear(s1, 16, 16)
+        clear(s2, 8, 8)
 
         for i, (dx, dy) in enumerate(NEAR):
             when_there(
                 dx, dy, lambda: block_copy("m", 0, dx, dy, i, len(NEAR), True).wait_recv()
             )
-        for c in range(2, 30):
+        for c in range(32):
             dx, k = (c - 8) // 16, (c - 8) % 16
             m0[c, 0:1, :] = mrx[dx + 1, 1, k : k + 1, :]
             m0[c, 1:2, :] = jnp.where(
@@ -289,28 +303,49 @@
             return scale if t == 0 else scale * halo_row
 
         def unpack_g(c, value):
-            g0[c, 1] = value
-
+            f0[c, 1] = value
+
+        profile_all(lambda dx, o: profile_copy(dx, o, True).wait_recv())
         wait_near(CYCLES, True)
         unpack(CYCLES, unpack_g)
+        centre0 = coefficients(0)[2]
+        strips = (
+            table[gy], table[jnp.minimum(gy + 1, n_gy - 1)], table[jnp.maximum(gy - 1, 0)]
+        )
+        for dx, first, k0, n in ((-1, 0, 8, 8), (0, 8, 0, 16), (1, 24, 0, 8)):
+            own, above, below = (prx[dx + 1, strip] for strip in strips)
+            for j in range(n):
+                c, k = first + j, k0 + j
+                column = slice(k, k + 1)
+                row = 16 + k
+                valid = column_in(c, 16, 8) * (WEIGHT / centre0)
+                g0[c, 0] = (f0[c, 0] + own[:, column] * mrx[dx + 1, 1, row : row + 1, :]) * (
+                    valid / m0[c, 0:1, :]
+                )
+                side = jnp.where(lane < 64, above[:, column], below[:, column])
+                steep = jnp.where(
+                    lane < 64, mrx[dx + 1, 2, row : row + 1, :], mrx[dx + 1, 0, row : row + 1, :]
+                )
+                g0[c, 1] = (f0[c, 1] + side * steep) * (valid * halo_row / m0[c, 1:2, :])
+
+        def g_copy(r, dx, dy, i, arriving):
+            return block_copy("g", r, dx, dy, i, len(FAR), arriving)
+
+        def far_all(action):
+            for i, (dx, dy) in enumerate(FAR):
+                when_there(dx, dy, lambda: action(dx, dy, i))
 
         sub = lax.broadcasted_iota(jnp.int32, (8, 128), 0)
 
         def cycle(r, carry):
             c0, c1, c2, c3 = (coefficients(level)[2] for level in range(4))
-            wait_near(r, False)
-
             def unpack_v(c, value):
                 v0[r, c, 1, 8:40, :] = value
-
-            unpack(r, unpack_v)
 
             def sweep0(c):
                 valid = column_in(c, 16, 8)
                 for t, (value, nb) in enumerate(around(v0, c, 32, 0, (r,))):
                     s0[c, t, 8:40, :] = 0.2 * value + weight_of(t, valid, 0) * nb + g0[c, t]
-
-            loop(1, 31, sweep0, 2)
 
             def residual0(c):
                 parts = [0.0, 0.0]
@@ -321,7 +356,21 @@
                 for t in range(2):
                     r0[c, t] = parts[t]
 
-            loop(1, 15, residual0)
+            wait_near(r, False, True)
+            unpack(r, unpack_v, (0,))
+            loop(9, 23, sweep0, 7)
+            loop(5, 11, residual0, 3)
+
+            @pl.when(r > 0)
+            def _():
+                far_all(lambda dx, dy, i: g_copy(r - 1, dx, dy, i, False).wait_send())
+
+            wait_near(r, False, False)
+            unpack(r, unpack_v, (-1, 1))
+            for low in (1, 23):
+                loop(low, low + 8, sweep0, 8)
+            for low in (1, 11):
+                loop(low, low + 4, residual0, 4)
 
             def restrict0(c):
                 for t in range(2):
@@ -330,7 +379,7 @@
                     g1[c, t] = g
                     s1[c, t, 8:24, :] = g
 
-            loop(1, 15, restrict0, 2)
+            loop(1, 15, restrict0, 7)
 
             def residual1(c):
                 parts = [0.0, 0.0]
@@ -341,7 +390,7 @@
                 for t in range(2):
                     r1[c, t] = parts[t]
 
-            loop(1, 7, residual1)
+            loop(1, 7, residual1, 3)
 
             def restrict1(c):
                 for t in range(2):
@@ -352,12 +401,8 @@
                 restrict1(c)
             for k in range(4):
                 own = s2[2 + k, 0, 8:16, :]
-                g2tx[r, k] = own
-                g2rx[r, 1, 1, k] = own
-            for i, (dx, dy) in enumerate(NEAR):
-                when_there(
-                    dx, dy, lambda: block_copy("g2", r, dx, dy, i, len(NEAR), False).start()
-                )
+                gtx[r, 8 * k : 8 * k + 8, :] = own
+                grx[r, REACH, 1, 8 * k : 8 * k + 8, :] = own
             for c in range(1, 3):
                 part = 0.0
                 for k in range(2):
@@ -367,16 +412,24 @@
                 r2[c - 1] = part
                 f = r2[c - 1, pl.ds(0, 4, stride=2), :] + r2[c - 1, pl.ds(1, 4, stride=2), :]
                 g = f * (0.25 * w3[c, 0:1, :])
-                g3tx[r, 4 * c - 4 : 4 * c, :] = g
-                g3rx[r, REACH, 1, 4 * c - 4 : 4 * c, :] = g
-            for i, (dx, dy) in enumerate(FAR):
-                when_there(
-                    dx, dy, lambda: block_copy("g3", r, dx, dy, i, len(FAR), False).start()
-                )
-            for i, (dx, dy) in enumerate(FAR):
-                when_there(
-                    dx, dy, lambda: block_copy("g3", r, dx, dy, i, len(FAR), True).wait_recv()
-                )
+                gtx[r, 28 + 4 * c : 32 + 4 * c, :] = g
+                grx[r, REACH, 1, 28 + 4 * c : 32 + 4 * c, :] = g
+            far_all(lambda dx, dy, i: g_copy(r, dx, dy, i, False).start())
+
+            for i, (dx, dy) in enumerate(NEAR):
+                when_there(dx, dy, lambda: near_copy(r, i, False, False).wait_send())
+
+            @pl.when(r == 0)
+            def _():
+                profile_all(lambda dx, o: profile_copy(dx, o, False).wait_send())
+                for i, (dx, dy) in enumerate(NEAR):
+                    def leave():
+                        block_copy("m", 0, dx, dy, i, len(NEAR), False).wait_send()
+                        near_copy(CYCLES, i, False, True).wait_send()
+
+                    when_there(dx, dy, leave)
+
+            far_all(lambda dx, dy, i: g_copy(r, dx, dy, i, True).wait_recv())
 
             kx, kz, _ = coefficients(3)
             width = 2 * REACH + 1
@@ -387,7 +440,10 @@
                 valid = jnp.where(there_x, WEIGHT / c3, 0.0).astype(jnp.float32)
                 scale3.append((valid, valid * halo_row))
                 gs.append(
-                    (g3rx[r, d, 1], jnp.where(lane < 64, g3rx[r, d, 2], g3rx[r, d, 0]))
+                    (
+                        grx[r, d, 1, 32:40, :],
+                        jnp.where(lane < 64, grx[r, d, 2, 32:40, :], grx[r, d, 0, 32:40, :]),
+                    )
                 )
             zero = jnp.zeros((8, 128), jnp.float32)
             vs = gs
@@ -420,16 +476,12 @@
                     p3[c, t, pl.ds(0, 4, stride=2), :] = column
                     p3[c, t, pl.ds(1, 4, stride=2), :] = column
 
-            for i, (dx, dy) in enumerate(NEAR):
-                when_there(
-                    dx, dy, lambda: block_copy("g2", r, dx, dy, i, len(NEAR), True).wait_recv()
-                )
-
             def g2_of(c):
-                dx, k = (c - 2) // 4, (c - 2) % 4
+                d, k = (c - 2) // 4 + REACH, (c - 2) % 4
+                rows = slice(8 * k, 8 * k + 8)
                 return (
-                    g2rx[r, dx + 1, 1, k],
-                    jnp.where(lane < 64, g2rx[r, dx + 1, 2, k], g2rx[r, dx + 1, 0, k]),
+                    grx[r, d, 1, rows, :],
+                    jnp.where(lane < 64, grx[r, d, 2, rows, :], grx[r, d, 0, rows, :]),
                 )
 
             for c in range(8):
@@ -449,7 +501,7 @@
                     for t in range(2):
                         s1[2 * c + k, t, 8:24, :] = g1[2 * c + k, t] + p2[c, t]
 
-            loop(1, 7, correct1, 2)
+            loop(1, 7, correct1, 6)
 
             def post1(c):
                 valid = column_in(c, 8, 4)
@@ -458,7 +510,7 @@
                     p1[c, t, pl.ds(0, 16, stride=2), :] = new
                     p1[c, t, pl.ds(1, 16, stride=2), :] = new
 
-            loop(3, 13, post1, 2)
+            loop(3, 13, post1, 5)
 
             def correct0(c):
                 for k in range(2):
@@ -466,17 +518,23 @@
                         old = s0[2 * c + k, t, 8:40, :]
                         s0[2 * c + k, t, 8:40, :] = old + p1[c, t]
 
-            loop(3, 13, correct0)
+            loop(3, 13, correct0, 2)
 
             def post0(c):
                 ((value, nb),) = around(s0, c, 32, 0, halo=False)
                 v0[r + 1, c, 0, 8:40, :] = 0.2 * value + (WEIGHT / c0) * nb + g0[c, 0]
 
-            loop(8, 24, post0, 2)
+            loop(8, 16, post0, 8)
 
             @pl.when(r + 1 < CYCLES)
             def _():
-                start_x(r + 1, False)
+                start_x(r + 1, False, (-1,))
+
+            loop(16, 24, post0, 8)
+
+            @pl.when(r + 1 < CYCLES)
+            def _():
+                start_x(r + 1, False, (1,))
                 start_y(r + 1, lambda k: v0[r + 1, 8 + k, 0, 8:40, :], False)
 
             return carry
@@ -486,23 +544,7 @@
         for x in range(16):
             out[pl.ds(x, 32, stride=16), :] = v0[CYCLES, 8 + x, 0, 8:40, :]
 
-        for o in range(1, n_gy):
-            profile_copy(o).wait_send()
-        for i, (dx, dy) in enumerate(NEAR):
-            def leave():
-                block_copy("m", 0, dx, dy, i, len(NEAR), False).wait_send()
-                for r in range(CYCLES + 1):
-                    near_copy(r, i, False, r == CYCLES).wait_send()
-                for r in range(CYCLES):
-                    block_copy("g2", r, dx, dy, i, len(NEAR), False).wait_send()
-
-            when_there(dx, dy, leave)
-        for i, (dx, dy) in enumerate(FAR):
-            def leave():
-                for r in range(CYCLES):
-                    block_copy("g3", r, dx, dy, i, len(FAR), False).wait_send()
-
-            when_there(dx, dy, leave)
+        far_all(lambda dx, dy, i: g_copy(CYCLES - 1, dx, dy, i, False).wait_send())
 
     return kernel
 
@@ -516,6 +558,7 @@
     shapes = [
         (CYCLES + 1, 32, 2, 48, 128),
         (32, 2, 48, 128),
+        (32, 2, 32, 128),
         (32, 2, 32, 128),
         (16, 2, 32, 128),
         (16, 2, 16, 128),
@@ -532,35 +575,36 @@
         (16, 8, 128),
         (8, 8, 128),
         (4, 8, 128),
-        (3, 3, 16, 128),
-        (n_gy, 32, 16),
+        (32, 128),
+        (3, 3, 32, 128),
+        (32, 16),
+        (3, n_gy, 32, 16),
         (CYCLES + 1, 32, 128),
         (CYCLES + 1, 3, 2, 32, 128),
-        (CYCLES, 4, 8, 128),
-        (CYCLES, 3, 3, 4, 8, 128),
-        (CYCLES, 8, 128),
-        (CYCLES, 2 * REACH + 1, 3, 8, 128),
+        (CYCLES, 40, 128),
+        (CYCLES, 2 * REACH + 1, 3, 40, 128),
+        (512, 128),
+        (512, 128),
     ]
     sems = [
         dma((CYCLES + 1, near)), dma((CYCLES + 1, near)), dma((near,)), dma((near,)),
-        dma((CYCLES, near)), dma((CYCLES, near)), dma((CYCLES, far)), dma((CYCLES, far)),
-        dma((n_gy,)), dma((n_gy,)),
+        dma((CYCLES, far)), dma((CYCLES, far)), dma((3, n_gy)), dma((3, n_gy)), dma((2,)),
     ]
     call = pl.pallas_call(
         make_kernel(n_gx, n_gy),
         out_shape=jax.ShapeDtypeStruct((512, 128), f32),
-        in_specs=[vmem] * 5 + [pl.BlockSpec(memory_space=pltpu.SMEM)],
+        in_specs=[pl.BlockSpec(memory_space=pltpu.HBM)] * 2 + [vmem] * 3 + [pl.BlockSpec(memory_space=pltpu.SMEM)],
         out_specs=vmem,
         scratch_shapes=[pltpu.VMEM(shape, f32) for shape in shapes] + sems,
         compiler_params=pltpu.CompilerParams(
-            collective_id=0, has_side_effects=True, vmem_limit_bytes=40 * 1024 * 1024
+            collective_id=0, has_side_effects=True, vmem_limit_bytes=62 * 1024 * 1024
         ),
     )
 
     def per_device(source, first_guess, metric, terrain_slope, profile_rows, profile_map):
         result = call(
             source.reshape(512, 128), first_guess.reshape(512, 128),
-            metric, terrain_slope, profile_rows, profile_map,
+            metric, terrain_slope, jnp.swapaxes(profile_rows, 1, 2), profile_map,
         )
         return result.reshape(source.shape)
 

time: 61.6 us -> 53.1 us (0.86)
  Pallas kernels: 57.9 us -> 50.9 us
  local copies, waits for them, and re-layouts: 3.42 us -> 1.67 us
    pallas_call x1, Pallas kernels: 57.9 us -> 50.9 us  [per_device(): call(source.reshape(512, 128), first_guess.reshape(512, 128), metric, ter...]
    unnamed x12 -> x1, local copies, waits for them, and re-layouts: 3.42 us -> 1.67 us
where the time goes in v2:
time: 53.1 us; the launch traced here: 52.6 us
  Pallas kernels  50.9 us (96%)
  local copies, waits for them, and re-layouts  1.67 us (3%)
    pallas_call x1, Pallas kernels, per_device(): call(source.reshape(512, 128), first_guess.reshape(512, 128), metric, ter...  50.9 us
    unnamed x1, local copies, waits for them, and re-layouts  1.67 us

profile of v2, /device:TPU:1, one launch (start us, length us, event | category | flops | bytes accessed | tf_op | source)
XLA Modules:
  0.0 52.6 jit_solution(9712743747032358345)
XLA Ops:
  0.0 50.9 %shard_map.64 = f32[512,128]{1,0:T(8,128)} custom-call(f32[512,128]{1,0:T(8,128)} %bitcast.5, f32[512,128]{1,0:T(8,128)} %bitcast.6, f32[16,128]{1,0:T(8,128)} %metric.1, f32[16,128]{1,0:T(8,128)} %slope.1, f32[1,16,32]{2,1,0:T(8,128)} %bitcast.7, s32[4]{0:T(128)} %table.1), custom_call_target="tpu_custom_call" | custom-call | tf_op jit(solution)/shard_map/pallas_call | solution.py:605
  51.0 1.7 %copy.8 = f32[1,32,16,128]{3,2,1,0:T(8,128)} copy(f32[1,32,16,128]{3,2,1,0:T(8,128)} %bitcast.4) | data formatting | bytes 524288

commit v3 on v2

--- a/solution.py
+++ b/solution.py
@@ -131,7 +131,7 @@
             @pl.when(jnp.logical_not(there(dx, dy)))
             def _():
                 for r in range(CYCLES):
-                    grx[r, dx + REACH, dy + 1] = jnp.zeros((40, 128), jnp.float32)
+                    grx[r, dx + REACH, dy + 1] = jnp.zeros((48, 128), jnp.float32)
 
         ptx[...] = profile[0].T
         prx[1, gy] = ptx[...]
@@ -191,7 +191,10 @@
                 src, dst = mtx, mrx.at[sx + 1, sy + 1]
                 ss, rs = metric_send.at[i], metric_recv.at[slot]
             else:
-                rows = pl.ds(0, 40) if abs(dx) < 2 else pl.ds(32, 8)
+                step = -dx if arriving else dx
+                rows = {-1: pl.ds(0, 24), 0: pl.ds(0, 40), 1: pl.ds(24, 24)}.get(
+                    step, pl.ds(0, 8)
+                )
                 src, dst = gtx.at[r, rows], grx.at[r, sx + REACH, sy + 1, rows]
                 ss, rs = g_send.at[r, i], g_recv.at[r, slot]
             return pltpu.make_async_remote_copy(
@@ -234,15 +237,15 @@
                     shift = (128 - (8 * (k0 + j) + 4)) % 128
                     store(first + j, pltpu.roll(both, shift, 1))
 
-        start_x(0, False)
-        start_x(CYCLES, True)
         profile_all(lambda dx, o: profile_copy(dx, o, False).start())
         for i, (dx, dy) in enumerate(NEAR):
             when_there(
                 dx, dy, lambda: block_copy("m", 0, dx, dy, i, len(NEAR), False).start()
             )
+        start_x(0, False)
+        start_x(CYCLES, True)
+        start_y(CYCLES, lambda k: f0[8 + k, 0], True)
         start_y(0, lambda k: v0[0, 8 + k, 0, 8:40, :], False)
-        start_y(CYCLES, lambda k: f0[8 + k, 0], True)
 
         for r in range(CYCLES):
             clear(v0, 32, 32, (r,))
@@ -305,28 +308,38 @@
         def unpack_g(c, value):
             f0[c, 1] = value
 
+        centre0 = coefficients(0)[2]
+
+        def right_side(parts):
+            for dx, first, k0, n in ((-1, 0, 8, 8), (0, 8, 0, 16), (1, 24, 0, 8)):
+                if dx not in parts:
+                    continue
+                own, above, below = (
+                    prx[dx + 1, strip]
+                    for strip in (
+                        table[gy],
+                        table[jnp.minimum(gy + 1, n_gy - 1)],
+                        table[jnp.maximum(gy - 1, 0)],
+                    )
+                )
+                for j in range(n):
+                    c, k = first + j, k0 + j
+                    column = slice(k, k + 1)
+                    row = 16 + k
+                    valid = column_in(c, 16, 8) * (WEIGHT / centre0)
+                    g0[c, 0] = (f0[c, 0] + own[:, column] * mrx[dx + 1, 1, row : row + 1, :]) * (
+                        valid / m0[c, 0:1, :]
+                    )
+                    side = jnp.where(lane < 64, above[:, column], below[:, column])
+                    steep = jnp.where(
+                        lane < 64, mrx[dx + 1, 2, row : row + 1, :], mrx[dx + 1, 0, row : row + 1, :]
+                    )
+                    g0[c, 1] = (f0[c, 1] + side * steep) * (valid * halo_row / m0[c, 1:2, :])
+
         profile_all(lambda dx, o: profile_copy(dx, o, True).wait_recv())
-        wait_near(CYCLES, True)
-        unpack(CYCLES, unpack_g)
-        centre0 = coefficients(0)[2]
-        strips = (
-            table[gy], table[jnp.minimum(gy + 1, n_gy - 1)], table[jnp.maximum(gy - 1, 0)]
-        )
-        for dx, first, k0, n in ((-1, 0, 8, 8), (0, 8, 0, 16), (1, 24, 0, 8)):
-            own, above, below = (prx[dx + 1, strip] for strip in strips)
-            for j in range(n):
-                c, k = first + j, k0 + j
-                column = slice(k, k + 1)
-                row = 16 + k
-                valid = column_in(c, 16, 8) * (WEIGHT / centre0)
-                g0[c, 0] = (f0[c, 0] + own[:, column] * mrx[dx + 1, 1, row : row + 1, :]) * (
-                    valid / m0[c, 0:1, :]
-                )
-                side = jnp.where(lane < 64, above[:, column], below[:, column])
-                steep = jnp.where(
-                    lane < 64, mrx[dx + 1, 2, row : row + 1, :], mrx[dx + 1, 0, row : row + 1, :]
-                )
-                g0[c, 1] = (f0[c, 1] + side * steep) * (valid * halo_row / m0[c, 1:2, :])
+        wait_near(CYCLES, True, True)
+        unpack(CYCLES, unpack_g, (0,))
+        right_side((0,))
 
         def g_copy(r, dx, dy, i, arriving):
             return block_copy("g", r, dx, dy, i, len(FAR), arriving)
@@ -365,6 +378,12 @@
             def _():
                 far_all(lambda dx, dy, i: g_copy(r - 1, dx, dy, i, False).wait_send())
 
+            @pl.when(r == 0)
+            def _():
+                wait_near(CYCLES, True, False)
+                unpack(CYCLES, unpack_g, (-1, 1))
+                right_side((-1, 1))
+
             wait_near(r, False, False)
             unpack(r, unpack_v, (-1, 1))
             for low in (1, 23):
@@ -401,8 +420,8 @@
                 restrict1(c)
             for k in range(4):
                 own = s2[2 + k, 0, 8:16, :]
-                gtx[r, 8 * k : 8 * k + 8, :] = own
-                grx[r, REACH, 1, 8 * k : 8 * k + 8, :] = own
+                gtx[r, 8 * k + 8 : 8 * k + 16, :] = own
+                grx[r, REACH, 1, 8 * k + 8 : 8 * k + 16, :] = own
             for c in range(1, 3):
                 part = 0.0
                 for k in range(2):
@@ -412,8 +431,9 @@
                 r2[c - 1] = part
                 f = r2[c - 1, pl.ds(0, 4, stride=2), :] + r2[c - 1, pl.ds(1, 4, stride=2), :]
                 g = f * (0.25 * w3[c, 0:1, :])
-                gtx[r, 28 + 4 * c : 32 + 4 * c, :] = g
-                grx[r, REACH, 1, 28 + 4 * c : 32 + 4 * c, :] = g
+                gtx[r, 4 * c - 4 : 4 * c, :] = g
+                gtx[r, 36 + 4 * c : 40 + 4 * c, :] = g
+                grx[r, REACH, 1, 4 * c - 4 : 4 * c, :] = g
             far_all(lambda dx, dy, i: g_copy(r, dx, dy, i, False).start())
 
             for i, (dx, dy) in enumerate(NEAR):
@@ -439,10 +459,11 @@
                 there_x = jnp.logical_and(gx + d - REACH >= 0, gx + d - REACH < n_gx)
                 valid = jnp.where(there_x, WEIGHT / c3, 0.0).astype(jnp.float32)
                 scale3.append((valid, valid * halo_row))
+                rows = slice(40, 48) if d == REACH - 1 else slice(0, 8)
                 gs.append(
                     (
-                        grx[r, d, 1, 32:40, :],
-                        jnp.where(lane < 64, grx[r, d, 2, 32:40, :], grx[r, d, 0, 32:40, :]),
+                        grx[r, d, 1, rows, :],
+                        jnp.where(lane < 64, grx[r, d, 2, rows, :], grx[r, d, 0, rows, :]),
                     )
                 )
             zero = jnp.zeros((8, 128), jnp.float32)
@@ -478,7 +499,7 @@
 
             def g2_of(c):
                 d, k = (c - 2) // 4 + REACH, (c - 2) % 4
-                rows = slice(8 * k, 8 * k + 8)
+                rows = slice(8 * k + 8, 8 * k + 16)
                 return (
                     grx[r, d, 1, rows, :],
                     jnp.where(lane < 64, grx[r, d, 2, rows, :], grx[r, d, 0, rows, :]),
@@ -581,8 +602,8 @@
         (3, n_gy, 32, 16),
         (CYCLES + 1, 32, 128),
         (CYCLES + 1, 3, 2, 32, 128),
-        (CYCLES, 40, 128),
-        (CYCLES, 2 * REACH + 1, 3, 40, 128),
+        (CYCLES, 48, 128),
+        (CYCLES, 2 * REACH + 1, 3, 48, 128),
         (512, 128),
         (512, 128),
     ]

time: 53.1 us -> 51.4 us (0.968)
  Pallas kernels: 50.9 us -> 49.6 us
    pallas_call x1, Pallas kernels: 50.9 us -> 49.6 us  [per_device(): call(source.reshape(512, 128), first_guess.reshape(512, 128), metric, ter...]
where the time goes in v3:
time: 51.4 us; the launch traced here: 51.2 us
  Pallas kernels  49.6 us (96%)
  local copies, waits for them, and re-layouts  1.67 us (3%)
    pallas_call x1, Pallas kernels, per_device(): call(source.reshape(512, 128), first_guess.reshape(512, 128), metric, ter...  49.6 us
    unnamed x1, local copies, waits for them, and re-layouts  1.67 us

profile of v3, /device:TPU:1, one launch (start us, length us, event | category | flops | bytes accessed | tf_op | source)
XLA Modules:
  0.0 51.2 jit_solution(3960989503886598117)
XLA Ops:
  0.0 49.6 %shard_map.64 = f32[512,128]{1,0:T(8,128)} custom-call(f32[512,128]{1,0:T(8,128)} %bitcast.5, f32[512,128]{1,0:T(8,128)} %bitcast.6, f32[16,128]{1,0:T(8,128)} %metric.1, f32[16,128]{1,0:T(8,128)} %slope.1, f32[1,16,32]{2,1,0:T(8,128)} %bitcast.7, s32[4]{0:T(128)} %table.1), custom_call_target="tpu_custom_call" | custom-call | tf_op jit(solution)/shard_map/pallas_call | solution.py:626
  49.6 1.7 %copy.8 = f32[1,32,16,128]{3,2,1,0:T(8,128)} copy(f32[1,32,16,128]{3,2,1,0:T(8,128)} %bitcast.4) | data formatting | bytes 524288

commit v4 on v3

--- a/solution.py
+++ b/solution.py
@@ -371,8 +371,8 @@
 
             wait_near(r, False, True)
             unpack(r, unpack_v, (0,))
-            loop(9, 23, sweep0, 7)
-            loop(5, 11, residual0, 3)
+            loop(9, 23, sweep0, 14)
+            loop(5, 11, residual0, 6)
 
             @pl.when(r > 0)
             def _():
@@ -398,7 +398,7 @@
                     g1[c, t] = g
                     s1[c, t, 8:24, :] = g
 
-            loop(1, 15, restrict0, 7)
+            loop(1, 15, restrict0, 14)
 
             def residual1(c):
                 parts = [0.0, 0.0]
@@ -409,7 +409,7 @@
                 for t in range(2):
                     r1[c, t] = parts[t]
 
-            loop(1, 7, residual1, 3)
+            loop(1, 7, residual1, 6)
 
             def restrict1(c):
                 for t in range(2):
@@ -531,7 +531,7 @@
                     p1[c, t, pl.ds(0, 16, stride=2), :] = new
                     p1[c, t, pl.ds(1, 16, stride=2), :] = new
 
-            loop(3, 13, post1, 5)
+            loop(3, 13, post1, 10)
 
             def correct0(c):
                 for k in range(2):

time: 51.4 us -> 50.4 us (0.981)
  Pallas kernels: 49.6 us -> 48.6 us
    pallas_call x1, Pallas kernels: 49.6 us -> 48.6 us  [per_device(): call(source.reshape(512, 128), first_guess.reshape(512, 128), metric, ter...]
where the time goes in v4:
time: 50.4 us; the launch traced here: 50.2 us
  Pallas kernels  48.6 us (96%)
  local copies, waits for them, and re-layouts  1.67 us (3%)
    pallas_call x1, Pallas kernels, per_device(): call(source.reshape(512, 128), first_guess.reshape(512, 128), metric, ter...  48.6 us
    unnamed x1, local copies, waits for them, and re-layouts  1.67 us

profile of v4, /device:TPU:1, one launch (start us, length us, event | category | flops | bytes accessed | tf_op | source)
XLA Modules:
  0.0 50.2 jit_solution(4255435093026067093)
XLA Ops:
  0.0 48.6 %shard_map.64 = f32[512,128]{1,0:T(8,128)} custom-call(f32[512,128]{1,0:T(8,128)} %bitcast.5, f32[512,128]{1,0:T(8,128)} %bitcast.6, f32[16,128]{1,0:T(8,128)} %metric.1, f32[16,128]{1,0:T(8,128)} %slope.1, f32[1,16,32]{2,1,0:T(8,128)} %bitcast.7, s32[4]{0:T(128)} %table.1), custom_call_target="tpu_custom_call" | custom-call | tf_op jit(solution)/shard_map/pallas_call | solution.py:626
  48.6 1.7 %copy.8 = f32[1,32,16,128]{3,2,1,0:T(8,128)} copy(f32[1,32,16,128]{3,2,1,0:T(8,128)} %bitcast.4) | data formatting | bytes 524288
